TPU v7x, 32 devices: a whole 2x2x4 slice. The times are simulated.
32 devices in a mesh: leaf: 2 (over core), row: 4 (over z), col: 4 (over y, x).
Axes of the slice: x: 2, y: 2, z: 4, core: 2. Of those that a mesh axis runs over, the one named last changes fastest.
Arguments:
- front: float32 [2, 16, 4, 128, 16, 4, 128], P('leaf', None, 'row', None, None, 'col'), as said below
- parent: float32 [8, 2, 4, 128, 16, 4, 128], P(None, 'leaf', 'row', None, None, 'col'), may hold values from -0.2 to 0.2
- tile_map: int32 [2, 56], replicated, may hold values from 0 to 63, as said below
- col_shift: int32 [16], replicated, may hold values from 0 to 3
Outputs:
- factored: float32 [2, 16, 4, 128, 16, 4, 128], P('leaf', None, 'row', None, None, 'col')
- new_parent: float32 [8, 2, 4, 128, 16, 4, 128], P(None, 'leaf', 'row', None, None, 'col')
Inputs may be any that keep to these rules, and one draw needn't show every extreme that they name: For each leaf the 8192 x 8192 matrix read from front is symmetric positive definite. Entry [l, e] names the parent tile joined by tile 8 + e of child l; no row repeats a value. The parent tile q = tile_map[l, e] has (q mod 4 + col_shift[q // 4]) mod 4 equal to (8 + e) mod 4. Among the tiles of one child whose indices are equal mod 4, at most 4 have parent tiles equal mod 8.
All inputs are finite; a program needn't handle non-finite values.
Results may differ from a plain program's by a relative error of at most 0.0001.
Values sent between devices are 32-bit elements; how exact they have to be, the bound alone decides.
A program may use at most 192 MiB of HBM per device.

v0:
```python
import jax
import jax.numpy as jnp
from jax import lax
from jax.sharding import PartitionSpec as P

TILE = 128
PB = 512
PANELS = 2
NPIV = 1024


HIGHEST = lax.Precision.HIGHEST


def spread(value, axis, source):
    kept = jnp.where(lax.axis_index(axis) == source, value, 0).astype(value.dtype)
    return lax.psum(kept, axis)


def update_slots(working, next_rows, column_factor, slot_low, slot_high):
    product = jnp.einsum(
        "atp,bsp->atbs",
        next_rows,
        column_factor,
        precision=HIGHEST,
        preferred_element_type=jnp.float32,
    )
    return working.at[:, :, slot_low:slot_high, :].add(-product)


def per_device(front, parent, tile_map, col_shift):
    leaf_count = lax.axis_size("leaf")
    row_count = lax.axis_size("row")
    col_count = lax.axis_size("col")
    leaf_index = lax.axis_index("leaf")
    row_index = lax.axis_index("row")
    col_index = lax.axis_index("col")
    local_front = front[0, :, 0, :, :, 0, :]
    row_slots = local_front.shape[0]
    col_slots = local_front.shape[2]
    panel_tiles = PB // TILE
    pivot_tiles = NPIV // TILE
    row_tiles = jnp.arange(row_slots, dtype=jnp.int32) * row_count + row_index
    col_tiles = jnp.arange(col_slots, dtype=jnp.int32) * col_count + col_index

    def fetch_panel(working, panel_index):
        pieces = []
        for offset in range(panel_tiles):
            column = panel_index * panel_tiles + offset
            column_tile = working[:, :, column // col_count, :]
            pieces.append(spread(column_tile, "col", column % col_count))
        return jnp.concatenate(pieces, axis=2)

    def write_factor(working, factor, panel_index):
        first_column = panel_index * panel_tiles
        slot_values = sorted(
            set([(first_column + offset) // col_count for offset in range(panel_tiles)])
        )
        for slot_index in slot_values:
            current = working[:, :, slot_index, :]
            for offset in range(panel_tiles):
                column = first_column + offset
                if column // col_count == slot_index:
                    current = jnp.where(
                        col_index == column % col_count,
                        factor[:, :, offset * TILE : (offset + 1) * TILE],
                        current,
                    )
            working = working.at[:, :, slot_index, :].set(current)
        return working

    working = local_front
    panel_block = fetch_panel(working, 0)
    for panel_index in range(PANELS):
        first_tile = panel_index * panel_tiles
        factor_slot_index = first_tile // row_count
        start_row = first_tile % row_count
        gathered = lax.all_gather(panel_block[factor_slot_index], "row", axis=0, tiled=True)
        diagonal_block = gathered[start_row * TILE : (start_row + panel_tiles) * TILE]
        lower_factor = jnp.linalg.cholesky(diagonal_block)
        factor_flattened = panel_block.reshape(row_slots * TILE, PB)
        solved = lax.linalg.triangular_solve(
            lower_factor, factor_flattened, left_side=False, lower=True, transpose_a=True
        )
        solved = solved.reshape(row_slots, TILE, PB)
        offset_tile = jnp.clip(row_index - start_row, 0, panel_tiles - 1)
        diagonal_rows = lax.dynamic_slice_in_dim(lower_factor, offset_tile * TILE, TILE, 0)
        in_panel = (row_tiles >= first_tile) & (row_tiles < first_tile + panel_tiles)
        factor_factor = jnp.where(in_panel[:, None, None], diagonal_rows[None], solved)
        factor_factor = jnp.where((row_tiles >= first_tile)[:, None, None], factor_factor, 0.0)
        next_rows = jnp.where(
            (row_tiles >= first_tile + panel_tiles)[:, None, None], factor_factor, 0.0
        )
        group_size = col_count // row_count
        owner_rows = spread(next_rows, "row", col_index % row_count)
        grouped = owner_rows.reshape(col_slots, group_size, TILE, PB)
        column_factor = lax.dynamic_index_in_dim(grouped, col_index // row_count, 1, keepdims=False)
        column_factor = jnp.where(
            (col_tiles >= first_tile + panel_tiles)[:, None, None], column_factor, 0.0
        )
        factor, next_rows, column_factor = (factor_factor, next_rows, column_factor)
        working = update_slots(working, next_rows, column_factor, 0, col_slots)
        upcoming = (
            fetch_panel(working, panel_index + 1) if panel_index + 1 < PANELS else panel_block
        )
        working = write_factor(working, factor, panel_index)
        panel_block = upcoming
    upper_part = (row_tiles < pivot_tiles)[:, None, None, None] & (col_tiles >= pivot_tiles)[
        None, None, :, None
    ]
    working = jnp.where(upper_part, 0.0, working)
    factored = working.reshape(front.shape)
    contribution = jnp.where((col_tiles >= pivot_tiles)[None, None, :, None], working, 0.0)
    contrib_count = tile_map.shape[1]
    entry_ids = jnp.arange(contrib_count, dtype=jnp.int32)
    own_map = lax.dynamic_index_in_dim(tile_map, leaf_index, 0, keepdims=False)
    row_match = (row_tiles - pivot_tiles)[:, None] == entry_ids[None, :]
    row_targets = jnp.sum(jnp.where(row_match, own_map[None, :], 0), axis=1)
    row_valid = row_tiles >= pivot_tiles
    owner_count = leaf_count * row_count
    destination = row_targets % owner_count
    parent_row_slot = row_targets // owner_count
    slot_ids = jnp.arange(row_slots, dtype=jnp.int32)
    same_before = (
        (destination[None, :] == destination[:, None])
        & row_valid[None, :]
        & (slot_ids[None, :] < slot_ids[:, None])
    )
    rank_in_dest = jnp.sum(same_before.astype(jnp.int32), axis=1)
    capacity = (col_slots + row_count - 1) // row_count
    owner_ids = jnp.arange(owner_count, dtype=jnp.int32)
    capacity_ids = jnp.arange(capacity, dtype=jnp.int32)
    selection = (
        row_valid[None, None, :]
        & (destination[None, None, :] == owner_ids[:, None, None])
        & (rank_in_dest[None, None, :] == capacity_ids[None, :, None])
    )
    flattened = contribution.reshape(row_slots, -1)
    send_buffer = jnp.einsum(
        "oka,ax->okx",
        selection.astype(jnp.float32),
        flattened,
        precision=HIGHEST,
        preferred_element_type=jnp.float32,
    )
    chosen_slot = jnp.sum(jnp.where(selection, parent_row_slot[None, None, :], 0), axis=2)
    send_slots = jnp.where(jnp.any(selection, axis=2), chosen_slot, -1)
    received, received_slots = (
        lax.all_to_all(send_buffer, ("leaf", "row"), split_axis=0, concat_axis=0, tiled=True),
        lax.all_to_all(send_slots, ("leaf", "row"), split_axis=0, concat_axis=0, tiled=True),
    )
    received = received.reshape(leaf_count, row_count, capacity, -1)
    received_slots = received_slots.reshape(leaf_count, row_count, capacity)
    parent_local = parent[:, 0, 0, :, :, 0, :]
    parent_rows = parent_local.shape[0]
    parent_cols = parent_local.shape[2]
    row_place = (
        received_slots[None] == jnp.arange(parent_rows, dtype=jnp.int32)[:, None, None, None]
    ).astype(jnp.float32)
    by_leaf = jnp.einsum(
        "slrk,lrkx->slx", row_place, received, precision=HIGHEST, preferred_element_type=jnp.float32
    )
    by_leaf = by_leaf.reshape(parent_rows, leaf_count, TILE, col_slots, TILE)
    col_match = (col_tiles - pivot_tiles)[:, None] == entry_ids[None, :]
    col_targets = jnp.sum(jnp.where(col_match[None], tile_map[:, None, :], 0), axis=2)
    col_valid = col_tiles >= pivot_tiles
    parent_slot_ids = jnp.arange(parent_cols, dtype=jnp.int32)
    col_place = (
        col_valid[None, None, :]
        & (col_targets[:, None, :] // col_count == parent_slot_ids[None, :, None])
    ).astype(jnp.float32)
    assembled = jnp.einsum(
        "sltbv,lub->stuv", by_leaf, col_place, precision=HIGHEST, preferred_element_type=jnp.float32
    )
    new_parent = (parent_local + assembled).reshape(parent.shape)
    return (factored, new_parent)


def solution(mesh):
    return jax.shard_map(
        per_device,
        mesh=mesh,
        in_specs=(
            P("leaf", None, "row", None, None, "col", None),
            P(None, "leaf", "row", None, None, "col", None),
            P(),
            P(),
        ),
        out_specs=(
            P("leaf", None, "row", None, None, "col", None),
            P(None, "leaf", "row", None, None, "col", None),
        ),
        check_vma=False,
    )
```

profile of v0, /device:TPU:11, one launch (start us, length us, event | category | flops | bytes accessed | tf_op | source)
XLA Modules:
  0.0 1969.3 jit_solution(12369998779616800720)
XLA Ops:
  7.2 39.8 %copy.77 = f32[1,16,1,128,16,1,128]{3,6,1,4,5,2,0:T(8,128)} copy(f32[1,16,1,128,16,1,128]{6,5,4,3,2,1,0:T(1,128)} %param.19) | data formatting | bytes 33554432 | tf_op args[0]
  47.0 3.4 select_bitcast_fusion.5
  50.5 106.2 %all-reduce.14.cloned.1.call-done = (f32[16,128,128]{1,2,0:T(8,128)}, f32[16,128,128]{1,2,0:T(8,128)}, f32[16,128,128]{1,2,0:T(8,128)}, f32[16,128,128]{1,2,0:T(8,128)}) async-done(((f32[16,128,128]{1,2,0:T(8,128)}, f32[16,128,128]{1,2,0:T(8,128)}, f32[16,128,128]{1,2,0:T(8,128)}, f32[16,128,128]{1,2,0:T(8,128)}), (f32[16,128,128]{1,2,0:T(8,128)}, f32[16,128,128]{1,2,0:T(8,128)}, f32[16,128,128]{1,2,0:T(8,128)}, ...) | async-done | bytes 4194320 | tf_op jit(solution)/shard_map/psum | solution.py:17
  162.7 5.4 copy.81
  168.1 22.7 %all-gather.5.cloned.1.call-done = f32[1,512,512]{1,2,0:T(8,128)} async-done(((f32[1,128,512]{1,2,0:T(8,128)}), f32[1,512,512]{1,2,0:T(8,128)}) %all-gather.5.cloned.1.call-update) | async-done | bytes 1048592 | tf_op jit(solution)/shard_map/all_gather | solution.py:78
  193.8 11.7 cholesky.286
  205.7 9.8 custom-call.27
  216.2 11.7 cholesky.305
  228.0 10.0 custom-call.28
  238.7 11.7 cholesky.326
  250.4 9.8 custom-call.29
  260.8 11.7 cholesky.343
  277.2 11.5 fusion.57
  288.7 7.8 while.10
  296.5 39.3 %custom-call.30 = f32[4,128,128]{1,2,0:T(8,128)S(1)} custom-call(f32[4,128,128]{2,1,0:T(8,128)S(1)} %get-tuple-element.82), custom_call_target="InvertDiagBlocksLowerTriangular" | custom-call | tf_op jit(solution)/shard_map/triangular_solve/custom-call.3 | solution.py:82
  335.8 2.4 fusion.52
  338.3 3.0 convolution_subtract_fusion.3
  342.4 3.5 convolution_subtract_fusion.1
  347.1 6.7 fusion.25
  357.7 2.5 broadcast_in_dim.236.clone
  360.2 5.4 copy.82
  365.6 5.8 pad_maximum_fusion
  371.4 5.3 copy.83
  376.8 5.4 copy.84
  382.1 6.7 select_select_fusion.4
  389.0 5.3 copy.114
  394.3 148.0 %all-reduce.8.cloned.1.call-done = f32[16,128,512]{1,2,0:T(8,128)} async-done(((f32[16,128,512]{1,2,0:T(8,128)}), f32[16,128,512]{1,2,0:T(8,128)}) %all-reduce.8.cloned.1.call-update) | async-done | bytes 4194320 | tf_op jit(solution)/shard_map/psum | solution.py:17
  542.4 33.9 %negate_add_fusion.1 = f32[16,128,16,128]{1,3,0,2:T(8,128)} fusion(f32[16,128,512,1]{2,1,0,3:T(8,128)} %bitcast.235, f32[16,128,512]{1,2,0:T(8,128)} %all-reduce.8.cloned.1.call-done, pred[16]{0:T(512)(128)(4,1)S(1)} %broadcast_compare_fusion.4, f32[1,16,1,128,16,1,128]{3,6,1,4,5,2,0:T(8,128)} %copy.77), kind=kOutput, calls=%fused_computation.9 | convolution fusion | flops 25779240960 | bytes 41943056 | tf_op jit(solution)/shard_map/atp,bsp->atbs/dot_general | solution.py:21
  576.2 4.2 select_bitcast_fusion.1
  580.5 105.9 %all-reduce.12.cloned.1.call-done = (f32[16,128,128]{1,2,0:T(8,128)}, f32[16,128,128]{1,2,0:T(8,128)}, f32[16,128,128]{1,2,0:T(8,128)}, f32[16,128,128]{1,2,0:T(8,128)}) async-done(((f32[16,128,128]{1,2,0:T(8,128)}, f32[16,128,128]{1,2,0:T(8,128)}, f32[16,128,128]{1,2,0:T(8,128)}, f32[16,128,128]{1,2,0:T(8,128)}), (f32[16,128,128]{1,2,0:T(8,128)}, f32[16,128,128]{1,2,0:T(8,128)}, f32[16,128,128]{1,2,0:T(8,128)}, ...) | async-done | bytes 4194320 | tf_op jit(solution)/shard_map/psum | solution.py:17
  692.5 5.5 copy.91
  698.0 22.7 %all-gather.7.cloned.1.call-done = f32[1,512,512]{1,2,0:T(8,128)} async-done(((f32[1,128,512]{1,2,0:T(8,128)}), f32[1,512,512]{1,2,0:T(8,128)}) %all-gather.7.cloned.1.call-update) | async-done | bytes 1048592 | tf_op jit(solution)/shard_map/all_gather | solution.py:78
  723.7 11.7 cholesky.358
  735.5 9.8 custom-call.31
  746.0 11.7 cholesky.377
  757.8 10.2 custom-call.32
  768.6 11.7 cholesky.398
  780.4 9.8 custom-call.33
  790.8 11.7 cholesky.415
  809.2 7.8 while.11
  817.1 39.3 %custom-call.34 = f32[4,128,128]{1,2,0:T(8,128)S(1)} custom-call(f32[4,128,128]{2,1,0:T(8,128)S(1)} %get-tuple-element.83), custom_call_target="InvertDiagBlocksLowerTriangular" | custom-call | tf_op jit(solution)/shard_map/triangular_solve/custom-call.3 | solution.py:82
  856.4 2.4 fusion.44
  858.8 3.0 convolution_subtract_fusion.2
  863.0 3.5 convolution_subtract_fusion
  867.6 6.7 fusion.22
  878.2 2.5 broadcast_in_dim.250.clone
  880.7 5.4 copy.92
  886.1 5.8 pad_maximum_fusion.1
  892.0 5.3 copy.93
  897.3 5.4 copy.94
  902.7 6.7 select_select_fusion.1
  911.5 4.9 all-to-all-start.1
  916.5 5.4 copy.117
  921.9 141.1 %all-reduce.10.cloned.1.call-done = f32[16,128,512]{1,2,0:T(8,128)} async-done(((f32[16,128,512]{1,2,0:T(8,128)}), f32[16,128,512]{1,2,0:T(8,128)}) %all-reduce.10.cloned.1.call-update) | async-done | bytes 4194320 | tf_op jit(solution)/shard_map/psum | solution.py:17
  1063.0 31.9 %negate_add_fusion = f32[16,128,16,128]{1,3,0,2:T(8,128)S(1)} fusion(f32[16,128,16,128]{1,3,0,2:T(8,128)} %get-tuple-element.133, f32[16,128,512,1]{2,1,0,3:T(8,128)} %bitcast.236, f32[16,128,512]{1,2,0:T(8,128)} %all-reduce.10.cloned.1.call-done, pred[16]{0:T(512)(128)(4,1)S(1)} %get-tuple-element.177), kind=kOutput, calls=%fused_computation.8 | convolution fusion | flops 25779240960 | bytes 41943056 | tf_op jit(solution)/shard_map/atp,bsp->atbs/dot_general | solution.py:21
  1095.6 11.6 select_select_fusion
  1107.2 17.6 copy.98
  1124.9 16.5 reshape.589
  1141.4 30.3 %fusion.95 = f32[8,4,262144]{2,1,0:T(4,128)} fusion(f32[16,262144,1]{1,0,2:T(8,128)} %reshape.589, pred[8,4,16]{2,0,1:T(8,128)(4,1)S(1)} %get-tuple-element.164), kind=kOutput, calls=%fused_computation.170 | convolution fusion | flops 1610612736 | bytes 50332160 | tf_op jit(solution)/shard_map/oka,ax->okx/dot_general | solution.py:139
  1171.7 9.8 all-to-all-start
  1181.8 39.8 %copy.104 = f32[1,16,1,128,16,1,128]{6,5,4,3,2,1,0:T(1,128)} copy(f32[1,16,1,128,16,1,128]{3,6,1,4,5,2,0:T(8,128)} %get-tuple-element.129) | data formatting | bytes 33554432
  1221.5 679.6 %all-to-all-done = f32[8,4,262144]{2,1,0:T(4,128)} async-done(((f32[8,4,262144]{2,1,0:T(4,128)}), f32[8,4,262144]{2,1,0:T(4,128)}, u32[]{:S(2)}, u32[]{:S(2)}) %all-to-all-start) | async-done | bytes 33554464 | tf_op jit(solution)/shard_map/all_to_all | solution.py:149
  1901.1 44.2 %fusion = f32[2,262144,8,1]{1,2,0,3:T(8,128)} fusion(f32[2,4,4,262144]{3,2,1,0:T(4,128)} %bitcast.61, s32[2,4,4]{1,0,2:T(2,128)S(1)} %copy.121), kind=kOutput, calls=%fused_computation.4 | convolution fusion | flops 805306624 | bytes 50331776 | tf_op jit(solution)/shard_map/slrk,lrkx->slx/dot_general | solution.py:160
  1945.3 16.8 bitcast_add_fusion
  (159 shorter events, 59.4 us)
Async XLA Ops:
  7.2 149.5 %all-reduce.14.cloned.1.call-start = ((), (), s32[]{:S(2)}) async-start(), calls=%async_computation.7 | async-start | bytes 8388608 | tf_op jit(solution)/shard_map/psum | solution.py:17
  50.4 140.4 %all-gather.5.cloned.1.call-start = ((), (), s32[]{:S(2)}) async-start(), calls=%async_computation.4 | async-start | bytes 1310720 | tf_op jit(solution)/shard_map/all_gather | solution.py:78
  156.6 2.8 copy-start.12
  156.6 2.9 copy-start.10
  159.6 2.0 copy-start.4
  162.4 379.9 %all-reduce.8.cloned.1.call-start = ((), (), s32[]{:S(2)}) async-start(), calls=%async_computation.2 | async-start | bytes 8388608 | tf_op jit(solution)/shard_map/psum | solution.py:17
  296.5 45.9 %copy-start.7 = (f32[512,512]{1,0:T(8,128)}, f32[512,512]{1,0:T(8,128)S(1)}, u32[]{:S(2)}) copy-start(f32[512,512]{1,0:T(8,128)S(1)} %get-tuple-element.308) | copy-start | bytes 3145732
  335.8 6.6 copy-start.2
  376.8 5.4 copy-start.9
  388.9 297.5 %all-reduce.12.cloned.1.call-start = ((), (), s32[]{:S(2)}) async-start(), calls=%async_computation.6 | async-start | bytes 8388608 | tf_op jit(solution)/shard_map/psum | solution.py:17
  542.4 33.9 %copy-start.1 = (f32[16,128,512]{1,2,0:T(8,128)S(1)}, f32[16,128,512]{1,2,0:T(8,128)}, u32[]{:S(2)}) copy-start(f32[16,128,512]{1,2,0:T(8,128)} %get-tuple-element.121) | copy-start | bytes 12582916
  580.5 140.2 %all-gather.7.cloned.1.call-start = ((), (), s32[]{:S(2)}) async-start(), calls=%async_computation.5 | async-start | bytes 1310720 | tf_op jit(solution)/shard_map/all_gather | solution.py:78
  686.5 2.8 copy-start.13
  686.5 2.9 copy-start.11
  689.5 2.0 copy-start.5
  692.2 370.7 %all-reduce.10.cloned.1.call-start = ((), (), s32[]{:S(2)}) async-start(), calls=%async_computation.3 | async-start | bytes 8388608 | tf_op jit(solution)/shard_map/psum | solution.py:17
  817.0 45.9 %copy-start.6 = (f32[512,512]{1,0:T(8,128)}, f32[512,512]{1,0:T(8,128)S(1)}, u32[]{:S(2)}) copy-start(f32[512,512]{1,0:T(8,128)S(1)} %get-tuple-element.307) | copy-start | bytes 3145732
  856.4 6.6 copy-start.3
  897.3 5.4 copy-start.8
  909.4 0.7 copy-start.14
  911.5 260.2 %all-to-all-start.1 = ((s32[8,1,4]{2,1,0:T(1,128)}), s32[8,1,4]{2,1,0:T(1,128)S(1)}, u32[]{:S(2)}, u32[]{:S(2)}) async-start(s32[8,1,4]{2,1,0:T(1,128)} %copy.101), calls=%async_computation.1 | async-start | bytes 8192 | tf_op jit(solution)/shard_map/all_to_all | solution.py:150
  1063.0 31.9 %copy-start = (f32[16,128,512]{1,2,0:T(8,128)S(1)}, f32[16,128,512]{1,2,0:T(8,128)}, u32[]{:S(2)}) copy-start(f32[16,128,512]{1,2,0:T(8,128)} %get-tuple-element.117) | copy-start | bytes 12582916
  1171.7 729.5 %all-to-all-start = ((f32[8,4,262144]{2,1,0:T(4,128)}), f32[8,4,262144]{2,1,0:T(4,128)}, u32[]{:S(2)}, u32[]{:S(2)}) async-start(f32[8,4,262144]{2,1,0:T(4,128)} %fusion.95), calls=%async_computation | async-start | bytes 67108864 | tf_op jit(solution)/shard_map/all_to_all | solution.py:149
Sparse Core Ops, SparseCore 0:
  50.5 106.0 all-reduce.13
  162.5 28.2 all-gather.4
  389.0 153.2 all-reduce.7
  580.6 105.8 all-reduce.11
  692.4 28.2 all-gather.6
  909.6 153.3 all-reduce.9
where the time goes:
time: 1990 us; the launch traced here: 1970 us
  waiting for transfers between devices  1230 us (62%)
  other arithmetic  299 us (15%)
  local copies, waits for them, and re-layouts  208 us (10%)
  matrix products  201 us (10%)
  between operations  20.3 us (1%)
    all_to_all x1, waiting for transfers between devices, per_device(): lax.all_to_all(send_buffer, ('leaf', 'row'), split_axis=0, concat_axis=0,...  680 us
    psum x4, waiting for transfers between devices, spread(): return lax.psum(kept, axis)  501 us
    another operation x29, other arithmetic, per_device(): lower_factor = jnp.linalg.cholesky(diagonal_block)  158 us
    another operation x7, other arithmetic, per_device(): lax.linalg.triangular_solve(lower_factor, factor_flattened, left_side=Fal...  103 us
    unnamed x38, local copies, waits for them, and re-layouts  90 us
    dot_general x2, matrix products, update_slots(): jnp.einsum('atp,bsp->atbs', next_rows, column_factor, precision=HIGHEST,...  65.8 us
    all_gather x2, waiting for transfers between devices, per_device(): lax.all_gather(panel_block[factor_slot_index], 'row', axis=0, tiled=True)  45.4 us
    dot_general x1, matrix products, per_device(): jnp.einsum('slrk,lrkx->slx', row_place, received, precision=HIGHEST, pref...  44.2 us
  transfers between devices with their start and end apart: 8, of which 7 were waited for; matrix products, arithmetic and copies ran while one was open for 9% of the time, Pallas kernels for 0%

commit v1 on v0

--- a/solution.py
+++ b/solution.py
@@ -1,6 +1,8 @@
 import jax
 import jax.numpy as jnp
 from jax import lax
+from jax.experimental import pallas as pl
+from jax.experimental.pallas import tpu as pltpu
 from jax.sharding import PartitionSpec as P
 
 TILE = 128
@@ -10,6 +12,7 @@
 
 
 HIGHEST = lax.Precision.HIGHEST
+HIGH = lax.Precision.HIGH
 
 
 def spread(value, axis, source):
@@ -176,9 +179,267 @@
     return (factored, new_parent)
 
 
+def factor_kernel(a_ref, lower_ref, inverse_ref, work, upper, small):
+    order = a_ref.shape[0]
+    blocks = order // TILE
+    tiles = TILE // 8
+    work[...] = a_ref[...]
+    lower_ref[...] = jnp.zeros_like(lower_ref)
+    inverse_ref[...] = jnp.zeros_like(inverse_ref)
+    lanes = lax.broadcasted_iota(jnp.int32, (8, TILE), 1)
+    subs = lax.broadcasted_iota(jnp.int32, (8, TILE), 0)
+    sub_column = lax.broadcasted_iota(jnp.int32, (8, 1), 0)
+
+    def dot(a, b, dims):
+        return lax.dot_general(
+            a, b, (dims, ((), ())), precision=HIGHEST, preferred_element_type=jnp.float32
+        )
+
+    def step(block, carry):
+        start = pl.multiple_of(block * TILE, TILE)
+        a = [work[pl.ds(start + 8 * i, 8), pl.ds(start, TILE)] for i in range(tiles)]
+        w = [jnp.where(lanes == subs + 8 * i, 1.0, 0.0).astype(jnp.float32) for i in range(tiles)]
+        for k in range(TILE):
+            home, sub = k // 8, k % 8
+            row_a = a[home][sub : sub + 1, :]
+            row_w = w[home][sub : sub + 1, :]
+            scale = lax.rsqrt(jnp.broadcast_to(row_a[:, k : k + 1], (1, TILE)))
+            row_a = row_a * scale
+            row_w = row_w * scale
+            for i in range(home, tiles):
+                column = jnp.broadcast_to(a[i][:, k : k + 1], (8, TILE)) * scale
+                if i == home:
+                    column = jnp.where(subs > sub, column, 0.0)
+                a[i] = a[i] - column * row_a
+                w[i] = w[i] - column * row_w
+            a[home] = jnp.where(subs == sub, row_a, a[home])
+            w[home] = jnp.where(subs == sub, row_w, w[home])
+        for i in range(tiles):
+            upper[8 * i : 8 * i + 8, :] = jnp.where(lanes >= subs + 8 * i, a[i], 0.0)
+            small[8 * i : 8 * i + 8, :] = w[i]
+        for b in range(blocks):
+
+            @pl.when(block == b)
+            def _():
+                low, high = b * TILE, (b + 1) * TILE
+                inv = small[...]
+                lower_ref[low:high, low:high] = upper[...].T
+                inverse_ref[low:high, low:high] = inv
+                if b:
+                    inverse_ref[low:high, :low] = dot(inv, inverse_ref[low:high, :low], ((1,), (0,)))
+                if b + 1 < blocks:
+                    below = dot(work[high:, low:high], inv, ((1,), (1,)))
+                    lower_ref[high:, low:high] = below
+                    work[high:, high:] -= dot(below, below, ((1,), (1,)))
+                    inverse_ref[high:, :high] -= dot(below, inverse_ref[low:high, :high], ((1,), (0,)))
+
+        return carry
+
+    lax.fori_loop(0, blocks, step, 0)
+
+
+def factor_leading(matrix):
+    order = matrix.shape[0]
+    shape = jax.ShapeDtypeStruct((order, order), jnp.float32)
+    return pl.pallas_call(
+        factor_kernel,
+        out_shape=(shape, shape),
+        in_specs=[pl.BlockSpec(memory_space=pltpu.VMEM)],
+        out_specs=(pl.BlockSpec(memory_space=pltpu.VMEM),) * 2,
+        scratch_shapes=[
+            pltpu.VMEM((order, order), jnp.float32),
+            pltpu.VMEM((TILE, TILE), jnp.float32),
+            pltpu.VMEM((TILE, TILE), jnp.float32),
+        ],
+        compiler_params=pltpu.CompilerParams(vmem_limit_bytes=56 * 1024 * 1024),
+        cost_estimate=pl.CostEstimate(
+            flops=4 * order**3, bytes_accessed=12 * order**2, transcendentals=0
+        ),
+        name="factor_leading",
+    )(matrix)
+
+
+def place_kernel(row_ids, col_ids, source_ref, out_ref):
+    row_id = row_ids[pl.program_id(0)]
+    for k in range(out_ref.shape[1] // TILE):
+        col_id = col_ids[k]
+        start = pl.multiple_of(jnp.maximum(col_id, 0) * TILE, TILE)
+        tile = source_ref[:, pl.ds(start, TILE)]
+        kept = (row_id >= 0) & (col_id >= 0)
+        out_ref[:, k * TILE : (k + 1) * TILE] = jnp.where(kept, tile, 0.0)
+
+
+def place(source, row_ids, col_ids):
+    rows, cols = row_ids.shape[0], col_ids.shape[0]
+    width = source.shape[1]
+    return pl.pallas_call(
+        place_kernel,
+        grid_spec=pltpu.PrefetchScalarGridSpec(
+            num_scalar_prefetch=2,
+            grid=(rows,),
+            in_specs=[pl.BlockSpec((TILE, width), lambda g, r, c: (jnp.maximum(r[g], 0), 0))],
+            out_specs=pl.BlockSpec((TILE, cols * TILE), lambda g, r, c: (g, 0)),
+        ),
+        out_shape=jax.ShapeDtypeStruct((rows * TILE, cols * TILE), jnp.float32),
+        compiler_params=pltpu.CompilerParams(vmem_limit_bytes=32 * 1024 * 1024),
+        cost_estimate=pl.CostEstimate(
+            flops=0, bytes_accessed=4 * rows * TILE * (width + cols * TILE), transcendentals=0
+        ),
+        name="place",
+    )(row_ids, col_ids, source)
+
+
+def add_kernel(row_ids, half, parent_ref, own_ref, other_ref, out_ref):
+    width = own_ref.shape[1]
+    own_cols = pl.ds(pl.multiple_of(half[0] * width, TILE), width)
+    other_cols = pl.ds(pl.multiple_of((1 - half[0]) * width, TILE), width)
+    out_ref[:, own_cols] = parent_ref[:, own_cols] + own_ref[...]
+    out_ref[:, other_cols] = parent_ref[:, other_cols] + other_ref[...]
+
+
+def add_rows(parent, own, other, row_ids, half):
+    rows, width = row_ids.shape[0], own.shape[1]
+    whole = pl.BlockSpec((TILE, 2 * width), lambda g, r, h: (g, 0))
+    return pl.pallas_call(
+        add_kernel,
+        grid_spec=pltpu.PrefetchScalarGridSpec(
+            num_scalar_prefetch=2,
+            grid=(rows,),
+            in_specs=[
+                whole,
+                pl.BlockSpec((TILE, width), lambda g, r, h: (r[g], 0)),
+                pl.BlockSpec((TILE, width), lambda g, r, h: (g, 0)),
+            ],
+            out_specs=whole,
+        ),
+        out_shape=jax.ShapeDtypeStruct(parent.shape, jnp.float32),
+        compiler_params=pltpu.CompilerParams(vmem_limit_bytes=32 * 1024 * 1024),
+        name="add_rows",
+    )(row_ids, half, parent, own, other)
+
+
+def per_device_square(front, parent, tile_map, col_shift):
+    side = lax.axis_size("row")
+    leaf_index = lax.axis_index("leaf")
+    row_index = lax.axis_index("row")
+    col_index = lax.axis_index("col")
+    x = front[0, :, 0, :, :, 0, :]
+    row_slots, _, col_slots, _ = x.shape
+    pivot_tiles = NPIV // TILE
+    first = pivot_tiles // side
+    rest_rows, rest_cols = row_slots - first, col_slots - first
+
+    leading = lax.all_gather(x[:first, :, :first, :], ("row", "col"))
+    leading = leading.reshape(side, side, first, TILE, first, TILE)
+    leading = leading.transpose(2, 0, 3, 4, 1, 5).reshape(NPIV, NPIV)
+    panel_rows = lax.all_gather(x[first:, :, :first, :], "col")
+    panel_rows = panel_rows.transpose(1, 2, 3, 0, 4).reshape(rest_rows * TILE, NPIV)
+    panel_cols = lax.all_gather(x[:first, :, first:, :], "row")
+    panel_cols = panel_cols.transpose(1, 0, 2, 3, 4).reshape(NPIV, rest_cols * TILE)
+
+    lower, inverse = factor_leading(leading)
+    row_factor = lax.dot_general(
+        panel_rows, inverse, (((1,), (1,)), ((), ())), precision=HIGH,
+        preferred_element_type=jnp.float32,
+    )
+    col_factor = lax.dot_general(
+        inverse, panel_cols, (((1,), (0,)), ((), ())), precision=HIGH,
+        preferred_element_type=jnp.float32,
+    )
+    rest = x[first:, :, first:, :].reshape(rest_rows * TILE, rest_cols * TILE)
+    rest = rest - lax.dot_general(
+        row_factor, col_factor, (((1,), (0,)), ((), ())), precision=HIGH,
+        preferred_element_type=jnp.float32,
+    )
+
+    slots = jnp.arange(col_slots, dtype=jnp.int32)
+    own_map = lax.dynamic_index_in_dim(tile_map, leaf_index, 0, keepdims=False)
+    own_slots = (own_map // side).reshape(-1, side)
+    row_target = lax.dynamic_index_in_dim(own_slots, row_index, 1, keepdims=False)
+    col_target = lax.dynamic_index_in_dim(own_slots, col_index, 1, keepdims=False)
+
+    def source_of(target):
+        match = target[None, :] == slots[:, None]
+        ids = jnp.arange(target.shape[0], dtype=jnp.int32)
+        return jnp.sum(jnp.where(match, ids[None, :] + 1, 0), axis=1) - 1
+
+    before = (col_shift[None, :] < col_shift[:, None]) | (
+        (col_shift[None, :] == col_shift[:, None]) & (slots[None, :] < slots[:, None])
+    )
+    rank = jnp.sum(before.astype(jnp.int32), axis=1)
+    in_order = (rank[None, :] == slots[:, None]).astype(jnp.int32)
+    row_source = jnp.sum(in_order * source_of(row_target)[None, :], axis=1)
+    sorted_shift = jnp.sum(in_order * col_shift[None, :], axis=1)
+    col_source = source_of(col_target).reshape(2, -1)
+    half = col_slots // 2
+
+    swap = [(0, 1), (1, 0)]
+    away = place(rest, row_source, col_source[1 - leaf_index])
+    came = lax.ppermute(away, "leaf", swap)
+    stays = place(rest, row_source, col_source[leaf_index])
+    summed = stays + came
+
+    share = col_slots // side
+
+    def by_groups(value):
+        pieces = [value[: share * TILE]]
+        for shift in range(1, side):
+            piece = value[shift * share * TILE : (shift + 1) * share * TILE]
+            perm = [(r, (r - shift) % side) for r in range(side)]
+            pieces.append(lax.ppermute(piece, "row", perm))
+        return jnp.concatenate(pieces, axis=0)
+
+    def by_gather(value):
+        everything = lax.all_gather(value, "row").reshape(side, col_slots, TILE, half * TILE)
+        pieces = []
+        for slot in range(col_slots):
+            origin = (row_index + sorted_shift[slot]) % side
+            pieces.append(lax.dynamic_index_in_dim(everything[:, slot], origin, 0, keepdims=False))
+        return jnp.concatenate(pieces, axis=0)
+
+    even = jnp.all(sorted_shift == slots // share)
+    rotated = lax.cond(even, by_groups, by_gather, summed)
+
+    position = rank.reshape(-1, 2)
+    across = place(
+        rotated,
+        lax.dynamic_index_in_dim(position, 1 - leaf_index, 1, keepdims=False),
+        jnp.arange(half, dtype=jnp.int32),
+    )
+    other = lax.ppermute(across, "leaf", swap)
+    parent_local = parent[:, 0, 0, :, :, 0, :].reshape(-1, col_slots * TILE)
+    new_parent = add_rows(
+        parent_local,
+        rotated,
+        other,
+        lax.dynamic_index_in_dim(position, leaf_index, 1, keepdims=False),
+        leaf_index.astype(jnp.int32)[None],
+    ).reshape(parent.shape)
+
+    own_rows = lax.dynamic_index_in_dim(
+        lower.reshape(first, side, TILE, first, side, TILE), row_index, 1, keepdims=False
+    )
+    own_corner = lax.dynamic_index_in_dim(own_rows, col_index, 3, keepdims=False)
+    own_below = lax.dynamic_index_in_dim(
+        row_factor.reshape(rest_rows, TILE, first, side, TILE), col_index, 3, keepdims=False
+    )
+    top = jnp.concatenate(
+        [own_corner, jnp.zeros((first, TILE, rest_cols, TILE), jnp.float32)], axis=2
+    )
+    bottom = jnp.concatenate(
+        [own_below, rest.reshape(rest_rows, TILE, rest_cols, TILE)], axis=2
+    )
+    factored = jnp.concatenate([top, bottom], axis=0).reshape(front.shape)
+    return (factored, new_parent)
+
+
 def solution(mesh):
+    sizes = dict(mesh.shape)
+    square = (
+        sizes["leaf"] == 2 and sizes["row"] == sizes["col"] and NPIV % (TILE * sizes["row"]) == 0
+    )
     return jax.shard_map(
-        per_device,
+        per_device_square if square else per_device,
         mesh=mesh,
         in_specs=(
             P("leaf", None, "row", None, None, "col", None),

time: 1990 us -> 722 us (0.36)
  waiting for transfers between devices: 1230 us -> 271 us
  other arithmetic: 299 us -> 29.1 us
  matrix products: 201 us -> 64.7 us
  Pallas kernels: 0 us -> 135 us
    all_to_all x2 -> x0, waiting for transfers between devices: 680 us -> none  [the longest x1 680 us: per_device(): lax.all_to_all(send_buffer, ('leaf', 'row'), split_axis=0, concat_axis=0,...]
    psum x4 -> x0, waiting for transfers between devices: 501 us -> none  [spread(): return lax.psum(kept, axis)]
    another operation x36 -> x0, other arithmetic: 261 us -> none  [the longest x29 158 us: per_device(): lower_factor = jnp.linalg.cholesky(diagonal_block)]
    ppermute x0 -> x5, waiting for transfers between devices: none -> 180 us  [the longest x3 179 us: by_groups(): pieces.append(lax.ppermute(piece, 'row', perm))]
    pallas_call x0 -> x5, Pallas kernels: none -> 135 us  [the longest x1 111 us: factor_leading(): pl.pallas_call(factor_kernel, out_shape=(shape, shape), in_specs=[pl.Bloc...]
    dot_general x5 -> x3, matrix products: 157 us -> 64.7 us  [the longest x1 30.8 us: per_device_square(): lax.dot_general(row_factor, col_factor, (((1,), (0,)), ((), ())), precisi...]
    reshape x3 -> x8, local copies, waits for them, and re-layouts: 27.2 us -> 78.5 us  [the longest x1 22.5 us: per_device_square(): leading = leading.reshape(side, side, first, TILE, first, TILE)]
    all_gather x2 -> x3, waiting for transfers between devices: 45.4 us -> 90.4 us  [the longest x1 52.5 us: per_device_square(): panel_cols = lax.all_gather(x[:first, :, first:, :], 'row')]
  transfers between devices with their start and end apart: 8 -> 8, of which waited for: 7 -> 6; matrix products, arithmetic and copies ran while one was open for 9% -> 21% of each run, Pallas kernels for 0% -> 16%
where the time goes in v1:
time: 722 us; the launch traced here: 715 us
  waiting for transfers between devices  271 us (38%)
  local copies, waits for them, and re-layouts  194 us (27%)
  Pallas kernels  135 us (19%)
  matrix products  64.7 us (9%)
  other arithmetic  29.1 us (4%)
  between operations  14.8 us (2%)
    ppermute x3, waiting for transfers between devices, by_groups(): pieces.append(lax.ppermute(piece, 'row', perm))  179 us
    pallas_call x1, Pallas kernels, factor_leading(): pl.pallas_call(factor_kernel, out_shape=(shape, shape), in_specs=[pl.Bloc...  111 us
    all_gather x1, waiting for transfers between devices, per_device_square(): panel_cols = lax.all_gather(x[:first, :, first:, :], 'row')  52.5 us
    unnamed x31, local copies, waits for them, and re-layouts  46.1 us
    all_gather x1, waiting for transfers between devices, per_device_square(): leading = lax.all_gather(x[:first, :, :first, :], ('row', 'col'))  37.9 us
    slice x2, local copies, waits for them, and re-layouts, per_device_square(): rest = x[first:, :, first:, :].reshape(rest_rows * TILE, rest_cols * TILE)  31 us
    dot_general x1, matrix products, per_device_square(): lax.dot_general(row_factor, col_factor, (((1,), (0,)), ((), ())), precisi...  30.8 us
    reshape x1, local copies, waits for them, and re-layouts, per_device_square(): leading = leading.reshape(side, side, first, TILE, first, TILE)  22.5 us
  transfers between devices with their start and end apart: 8, of which 6 were waited for; matrix products, arithmetic and copies ran while one was open for 21% of the time, Pallas kernels for 16%

profile of v1, /device:TPU:11, one launch (start us, length us, event | category | flops | bytes accessed | tf_op | source)
XLA Modules:
  0.0 715.0 jit_solution(9334623055242790850)
XLA Ops:
  7.2 0.0 copy-start
  7.2 0.0 all-gather.11.cloned.1.call-start
  7.2 10.9 %copy.35 = f32[1,16,1,128,16,1,128]{6,3,4,1,5,2,0:T(8,128)S(1)} copy(f32[1,16,1,128,16,1,128]{6,5,4,3,2,1,0:T(1,128)} %param.6) | data formatting | bytes 33554432 | tf_op args[0]
  18.1 0.0 copy-start.5
  18.1 6.2 copy-done.5
  24.3 0.7 slice.140
  25.0 0.0 all-gather.11.cloned.1.call-update
  25.0 0.0 all-gather.13.cloned.1.call-start
  25.1 2.9 slice.141
  28.0 0.0 all-gather.13.cloned.1.call-update
  28.0 0.4 all-gather.15.cloned.1.call-start
  28.5 3.0 slice.143
  31.4 0.0 all-gather.15.cloned.1.call-update
  31.5 11.7 %slice.142 = f32[14,128,14,128]{3,1,2,0:T(8,128)} slice(f32[16,128,16,128]{3,1,2,0:T(8,128)} %bitcast.104), slice={[2:16], [0:128], [2:16], [0:128]} | slice | bytes 25690112 | tf_op jit(solution)/shard_map/slice | solution.py:349
  43.2 0.1 squeeze.150
  43.3 0.2 dynamic-slice_reduce_fusion
  43.5 0.1 select_reduce_fusion
  43.6 0.1 sub.30
  43.7 19.3 %copy.23 = f32[14,128,14,128]{3,2,1,0:T(8,128)} copy(f32[14,128,14,128]{3,1,2,0:T(8,128)} %slice.142) | data formatting | bytes 25690112 | tf_op jit(solution)/shard_map/slice | solution.py:349
  63.0 0.2 convert_reduce_fusion
  63.2 0.1 select_reduce_fusion.1
  63.3 37.9 %all-gather.11.cloned.1.call-done = f32[32,128,2,128]{3,1,2,0:T(8,128)} async-done(((f32[2,128,2,128]{3,1,2,0:T(8,128)}), f32[32,128,2,128]{3,1,2,0:T(8,128)}) %all-gather.11.cloned.1.call-update) | async-done | bytes 4194320 | tf_op jit(solution)/shard_map/all_gather | solution.py:332
  101.2 22.5 %copy.38 = f32[4,4,2,128,2,128]{5,1,4,3,0,2:T(4,128)} copy(f32[4,4,2,128,2,128]{5,3,4,2,1,0:T(8,128)} %bitcast.118) | data formatting | bytes 8388608 | tf_op jit(solution)/shard_map/reshape | solution.py:333
  123.8 5.5 reshape.96.a_ref
  129.2 111.2 %factor_leading.1 = (f32[1024,1024]{1,0:T(8,128)}, f32[1024,1024]{1,0:T(8,128)}) custom-call(f32[1024,1024]{1,0:T(8,128)} %reshape.96.a_ref), custom_call_target="tpu_custom_call" | custom-call | flops 4294967296 | bytes 12582912 | tf_op jit(solution)/shard_map/factor_leading/pallas_call | solution.py:244
  240.4 10.9 %copy.37 = f32[4,14,128,2,128]{4,0,3,2,1:T(4,128)} copy(f32[4,14,128,2,128]{4,2,3,1,0:T(8,128)} %bitcast.115) | data formatting | bytes 14680064 | tf_op jit(solution)/shard_map/all_gather | solution.py:335
  251.4 9.9 %reshape.98 = f32[1792,1024]{1,0:T(8,128)} reshape(f32[14,128,2,4,128]{4,3,2,1,0:T(4,128)} %bitcast.106) | data formatting | bytes 14680064 | tf_op jit(solution)/shard_map/reshape | solution.py:336
  261.2 52.5 %all-gather.15.cloned.1.call-done = f32[8,128,14,128]{3,1,2,0:T(8,128)} async-done(((f32[2,128,14,128]{3,1,2,0:T(8,128)}), f32[8,128,14,128]{3,1,2,0:T(8,128)}) %all-gather.15.cloned.1.call-update) | async-done | bytes 7340048 | tf_op jit(solution)/shard_map/all_gather | solution.py:337
  313.8 9.5 %copy.24 = f32[4,2,128,14,128]{2,0,1,4,3:T(4,128)} copy(f32[4,2,128,14,128]{4,2,3,1,0:T(8,128)} %bitcast.116) | data formatting | bytes 14680064 | tf_op jit(solution)/shard_map/all_gather | solution.py:337
  323.3 9.8 %reshape.101 = f32[1024,1792]{0,1:T(8,128)} reshape(f32[2,4,128,14,128]{2,1,0,4,3:T(4,128)} %bitcast.107) | data formatting | bytes 14680064 | tf_op jit(solution)/shard_map/reshape | solution.py:338
  333.1 16.7 %fusion.10 = f32[1792,1024]{1,0:T(8,128)} fusion(f32[1792,1024]{1,0:T(8,128)} %reshape.98, f32[1024,1024]{1,0:T(8,128)} %get-tuple-element.18), kind=kOutput, calls=%fused_computation.65 | convolution fusion | flops 11274289152 | bytes 18874368 | tf_op jit(solution)/shard_map/dot_general | solution.py:341
  349.8 17.3 %fusion.11 = f32[1024,1792]{1,0:T(8,128)} fusion(f32[1024,1024]{1,0:T(8,128)S(1)} %copy-done.7, f32[1024,1792]{0,1:T(8,128)} %reshape.101), kind=kOutput, calls=%fused_computation.66 | convolution fusion | flops 11274289152 | bytes 18874368 | tf_op jit(solution)/shard_map/dot_general | solution.py:345
  367.1 30.8 %bitcast_subtract_fusion.source_ref = f32[1792,1792]{1,0:T(8,128)} fusion(f32[224,8,14,128]{3,2,1,0:T(8,128)S(1)} %bitcast.112, f32[1792,1024]{1,0:T(8,128)} %fusion.10, f32[1024,1792]{1,0:T(8,128)} %fusion.11), kind=kOutput, calls=%fused_computation.20 | convolution fusion | flops 19733217280 | bytes 40370176 | tf_op jit(solution)/shard_map/dot_general | solution.py:350
  397.9 4.6 copy-done.2
  402.6 8.0 %place.4 = f32[2048,1024]{1,0:T(8,128)} custom-call(s32[16]{0:T(128)S(1)} %get-tuple-element.33.row_ids, s32[8]{0:T(128)S(1)} %get-tuple-element.71.col_ids, f32[1792,1792]{1,0:T(8,128)S(1)} %copy-done.2), custom_call_target="tpu_custom_call" | custom-call | bytes 23068672 | tf_op jit(solution)/shard_map/place/pallas_call | solution.py:275
  410.6 0.7 collective-permute-start.3
  411.3 0.1 reshape.104
  411.4 0.6 compare_reduce_fusion
  412.7 0.2 dynamic-slice_reduce_fusion.2
  412.9 4.6 copy-done.3
  417.6 2.0 place.3
  419.5 3.4 copy-done.4
  422.9 1.5 collective-permute-done.3
  424.4 12.1 %add.212 = f32[2048,1024]{1,0:T(8,128)} add(f32[2048,1024]{1,0:T(8,128)} %copy-done.4, f32[2048,1024]{1,0:T(8,128)} %collective-permute-done.3) | non-fusion elementwise | flops 2097152 | bytes 25165824 | tf_op jit(solution)/shard_map/add | solution.py:380
  436.6 191.5 %conditional.1 = (f32[2048,1024]{1,0:T(8,128)}) conditional(s32[]{:T(128)} %convert_element_type.8, (f32[2048,1024]{1,0:T(8,128)}, s32[16]{0:T(128)S(1)}, s32[]{:T(128)}) %tuple.14, f32[2048,1024]{1,0:T(8,128)} %add.212), branch_computations={%region_6.7_spmd, %region_7.8_spmd} | conditional | flops 6291456 | bytes 209718432 | solution.py:401
  436.6 4.3 fusion.9
  440.9 3.1 collective-permute-start
  444.0 0.4 collective-permute-start.1
  444.3 1.1 collective-permute-start.2
  445.4 43.5 %collective-permute-done = f32[512,1024]{1,0:T(8,128)S(1)} collective-permute-done((f32[512,1024]{1,0:T(8,128)S(1)}, f32[512,1024]{1,0:T(8,128)S(1)}, u32[]{:S(2)}, u32[]{:S(2)}) %collective-permute-start) | collective-permute-done | bytes 2097184 | tf_op jit(solution)/shard_map/cond/branch_1_fun/ppermute | solution.py:389
  488.9 90.3 %collective-permute-done.1 = f32[512,1024]{1,0:T(8,128)S(1)} collective-permute-done((f32[512,1024]{1,0:T(8,128)S(1)}, f32[512,1024]{1,0:T(8,128)S(1)}, u32[]{:S(2)}, u32[]{:S(2)}) %collective-permute-start.1) | collective-permute-done | bytes 2097184 | tf_op jit(solution)/shard_map/cond/branch_1_fun/ppermute | solution.py:389
  579.2 44.9 %collective-permute-done.2 = f32[512,1024]{1,0:T(8,128)S(1)} collective-permute-done((f32[512,1024]{1,0:T(8,128)S(1)}, f32[512,1024]{1,0:T(8,128)S(1)}, u32[]{:S(2)}, u32[]{:S(2)}) %collective-permute-start.2) | collective-permute-done | bytes 2097184 | tf_op jit(solution)/shard_map/cond/branch_1_fun/ppermute | solution.py:389
  624.2 3.9 pad_maximum_fusion
  628.1 7.4 %place.5 = f32[1024,1024]{1,0:T(8,128)} custom-call(s32[8]{0:T(128)S(1)} %get-tuple-element.29.row_ids, s32[8]{0:T(128)S(1)} %iota.23.col_ids, f32[2048,1024]{1,0:T(8,128)} %get-tuple-element.75.source_ref.own_ref), custom_call_target="tpu_custom_call" | custom-call | bytes 8388608 | tf_op jit(solution)/shard_map/place/pallas_call | solution.py:275
  635.5 0.5 collective-permute-start.4
  636.0 10.9 %copy.36 = f32[128,8,16,128]{3,1,2,0:T(8,128)} copy(f32[128,8,16,128]{3,2,1,0:T(8,128)} %bitcast.113) | data formatting | bytes 16777216
  646.9 5.6 reshape.97
  652.5 1.5 constant_dynamic-slice_fusion.4
  654.0 10.1 %reshape.99 = f32[14,128,2,4,128]{4,3,2,1,0:T(4,128)} reshape(f32[1792,1024]{1,0:T(8,128)} %fusion.10) | data formatting | bytes 14680064 | tf_op jit(solution)/shard_map/reshape | solution.py:424
  664.1 15.0 %reshape.102 = f32[14,128,14,128]{3,2,1,0:T(8,128)} reshape(f32[1792,1792]{1,0:T(8,128)} %bitcast_subtract_fusion.source_ref) | data formatting | bytes 25690112 | tf_op jit(solution)/shard_map/reshape | solution.py:430
  679.1 5.2 constant_dynamic-slice_fusion.3
  684.3 11.9 %select_maximum_fusion = f32[16,128,16,128]{3,2,1,0:T(8,128)} fusion(f32[2,128,2,128]{3,2,1,0:T(2,128)S(1)} %bitcast.119, f32[14,128,14,128]{3,2,1,0:T(8,128)} %reshape.102, f32[14,128,2,128]{3,2,1,0:T(2,128)S(1)} %bitcast.117), kind=kLoop, calls=%fused_computation.17 | loop fusion | flops 16777216 | bytes 31719424 | tf_op jit(solution)/shard_map/concatenate | solution.py:432
  696.2 6.6 add_rows.1
  702.9 5.4 copy.29
  (32 shorter events, 0.1 us)
Async XLA Ops:
  7.2 36.0 %copy-start = (s32[2,56]{1,0:T(2,128)S(1)}, s32[2,56]{1,0:T(2,128)}, u32[]{:S(2)}) copy-start(s32[2,56]{1,0:T(2,128)} %param.8) | copy-start | bytes 1348
  7.2 94.0 %all-gather.11.cloned.1.call-start = ((), (), s32[]{:S(2)}) async-start(), calls=%async_computation.1 | async-start | bytes 4456448 | tf_op jit(solution)/shard_map/all_gather | solution.py:332
  18.1 6.2 copy-start.5
  25.0 215.4 %all-gather.13.cloned.1.call-start = ((), (), s32[]{:S(2)}) async-start(), calls=%async_computation.2 | async-start | bytes 9175040 | tf_op jit(solution)/shard_map/all_gather | solution.py:335
  28.0 285.7 %all-gather.15.cloned.1.call-start = ((), (), s32[]{:S(2)}) async-start(), calls=%async_computation.3 | async-start | bytes 9175040 | tf_op jit(solution)/shard_map/all_gather | solution.py:337
  43.7 19.3 %copy-start.6 = (s32[16]{0:T(128)S(1)}, s32[16]{0:T(128)}, u32[]{:S(2)}) copy-start(s32[16]{0:T(128)} %param.9) | copy-start | bytes 196
  333.1 16.7 %copy-start.7 = (f32[1024,1024]{1,0:T(8,128)S(1)}, f32[1024,1024]{1,0:T(8,128)}, u32[]{:S(2)}) copy-start(f32[1024,1024]{1,0:T(8,128)} %get-tuple-element.18) | copy-start | bytes 12582916
  333.1 34.0 %slice-start.2 = ((s8[14680064]{0:T(1024)(128)(4,1)}), s8[4194304]{0:T(1024)(128)(4,1)S(1)}, s32[]{:S(2)}) async-start(s8[14680064]{0:T(1024)(128)(4,1)} %bitcast.110), calls=%async_computation.6 | async-start | bytes 8388608
  333.1 34.0 %slice-start.3 = ((s8[14680064]{0:T(1024)(128)(4,1)}), s8[4194304]{0:T(1024)(128)(4,1)S(1)}, s32[]{:S(2)}) async-start(s8[14680064]{0:T(1024)(128)(4,1)} %bitcast.110), calls=%async_computation.7 | async-start | bytes 8388608
  349.8 17.3 %slice-start.4 = ((s8[14680064]{0:T(1024)(128)(4,1)}), s8[4194304]{0:T(1024)(128)(4,1)S(1)}, s32[]{:S(2)}) async-start(s8[14680064]{0:T(1024)(128)(4,1)} %bitcast.110), calls=%async_computation.8 | async-start | bytes 8388608
  349.8 17.3 %slice-start.5 = ((s8[14680064]{0:T(1024)(128)(4,1)}), s8[2097152]{0:T(1024)(128)(4,1)S(1)}, s32[]{:S(2)}) async-start(s8[14680064]{0:T(1024)(128)(4,1)} %bitcast.110), calls=%async_computation.9 | async-start | bytes 4194304
  397.9 4.7 copy-start.2
  410.6 13.9 %collective-permute-start.3 = (f32[2048,1024]{1,0:T(8,128)}, f32[2048,1024]{1,0:T(8,128)}, u32[]{:S(2)}, u32[]{:S(2)}) collective-permute-start(f32[2048,1024]{1,0:T(8,128)} %place.4), channel_id=1, source_target_pairs={{0,16},{16,0},{1,17},{17,1},{2,18},{18,2},{3,19},{19,3},{4,20},{20... | collective-permute-start | bytes 25165832 | tf_op jit(solution)/shard_map/ppermute | solution.py:378
  412.9 4.7 copy-start.3
  419.5 3.4 copy-start.4
  440.9 48.0 %collective-permute-start = (f32[512,1024]{1,0:T(8,128)S(1)}, f32[512,1024]{1,0:T(8,128)S(1)}, u32[]{:S(2)}, u32[]{:S(2)}) collective-permute-start(f32[512,1024]{1,0:T(8,128)S(1)} %get-tuple-element.70), channel_id=1, source_target_pairs={{0,12},{4,0},{8,4},{12,8},{1,13},{5,1},{9,5},{13,9},{2,14},{6,2},{... | collective-permute-start | bytes 6291464 | tf_op jit(solution)/shard_map/cond/branch_1_fun/ppermute | solution.py:389
  444.0 135.3 %collective-permute-start.1 = (f32[512,1024]{1,0:T(8,128)S(1)}, f32[512,1024]{1,0:T(8,128)S(1)}, u32[]{:S(2)}, u32[]{:S(2)}) collective-permute-start(f32[512,1024]{1,0:T(8,128)S(1)} %get-tuple-element.69), channel_id=1, source_target_pairs={{0,8},{4,12},{8,0},{12,4},{1,9},{5,13},{9,1},{13,5},{2,10},{6,14},... | collective-permute-start | bytes 6291464 | tf_op jit(solution)/shard_map/cond/branch_1_fun/ppermute | solution.py:389
  444.3 179.8 %collective-permute-start.2 = (f32[512,1024]{1,0:T(8,128)S(1)}, f32[512,1024]{1,0:T(8,128)S(1)}, u32[]{:S(2)}, u32[]{:S(2)}) collective-permute-start(f32[512,1024]{1,0:T(8,128)S(1)} %get-tuple-element.68), channel_id=1, source_target_pairs={{0,4},{4,8},{8,12},{12,0},{1,5},{5,9},{9,13},{13,1},{2,6},{6,10},{... | collective-permute-start | bytes 6291464 | tf_op jit(solution)/shard_map/cond/branch_1_fun/ppermute | solution.py:389
  635.5 60.8 %collective-permute-start.4 = (f32[1024,1024]{1,0:T(8,128)}, f32[1024,1024]{1,0:T(8,128)}, u32[]{:S(2)}, u32[]{:S(2)}) collective-permute-start(f32[1024,1024]{1,0:T(8,128)} %place.5), channel_id=1, source_target_pairs={{0,16},{16,0},{1,17},{17,1},{2,18},{18,2},{3,19},{19,3},{4,20},{20... | collective-permute-start | bytes 12582920 | tf_op jit(solution)/shard_map/ppermute | solution.py:409
  679.1 17.1 %slice-start = ((s8[8388608]{0:T(1024)(128)(4,1)}), s8[4194304]{0:T(1024)(128)(4,1)S(1)}, s32[]{:S(2)}) async-start(s8[8388608]{0:T(1024)(128)(4,1)} %bitcast.97), calls=%async_computation.4 | async-start | bytes 8388608
  684.3 12.0 %slice-start.1 = ((s8[8388608]{0:T(1024)(128)(4,1)}), s8[4194304]{0:T(1024)(128)(4,1)S(1)}, s32[]{:S(2)}) async-start(s8[8388608]{0:T(1024)(128)(4,1)} %bitcast.97), calls=%async_computation.5 | async-start | bytes 8388608
  702.9 5.4 copy-start.1
Sparse Core Ops, SparseCore 0:
  25.2 76.0 all-gather.10
  103.1 79.5 all-gather.12
  184.2 129.5 all-gather.14

commit v2 on v1

--- a/solution.py
+++ b/solution.py
@@ -332,18 +332,32 @@
     leading = lax.all_gather(x[:first, :, :first, :], ("row", "col"))
     leading = leading.reshape(side, side, first, TILE, first, TILE)
     leading = leading.transpose(2, 0, 3, 4, 1, 5).reshape(NPIV, NPIV)
-    panel_rows = lax.all_gather(x[first:, :, :first, :], "col")
-    panel_rows = panel_rows.transpose(1, 2, 3, 0, 4).reshape(rest_rows * TILE, NPIV)
-    panel_cols = lax.all_gather(x[:first, :, first:, :], "row")
-    panel_cols = panel_cols.transpose(1, 0, 2, 3, 4).reshape(NPIV, rest_cols * TILE)
+    panel_rows = x[first:, :, :first, :].reshape(rest_rows * TILE, first * TILE)
+    panel_rows = lax.all_gather(panel_rows, "col", axis=1, tiled=True)
+    own_cols = x[:first, :, first:, :].reshape(first * TILE, rest_cols * TILE)
+    pieces = [own_cols]
+    for shift in range(1, side):
+        perm = [(r, (r - shift) % side) for r in range(side)]
+        pieces.append(lax.ppermute(own_cols, "row", perm))
+    panel_cols = jnp.concatenate(pieces, axis=0)
 
     lower, inverse = factor_leading(leading)
+    by_col = [
+        inverse[:, (b * side + c) * TILE : (b * side + c + 1) * TILE]
+        for c in range(side)
+        for b in range(first)
+    ]
+    by_row = [
+        lax.dynamic_slice_in_dim(inverse, (a * side + (row_index + shift) % side) * TILE, TILE, 1)
+        for shift in range(side)
+        for a in range(first)
+    ]
     row_factor = lax.dot_general(
-        panel_rows, inverse, (((1,), (1,)), ((), ())), precision=HIGH,
+        panel_rows, jnp.concatenate(by_col, axis=1), (((1,), (1,)), ((), ())), precision=HIGH,
         preferred_element_type=jnp.float32,
     )
     col_factor = lax.dot_general(
-        inverse, panel_cols, (((1,), (0,)), ((), ())), precision=HIGH,
+        jnp.concatenate(by_row, axis=1), panel_cols, (((1,), (0,)), ((), ())), precision=HIGH,
         preferred_element_type=jnp.float32,
     )
     rest = x[first:, :, first:, :].reshape(rest_rows * TILE, rest_cols * TILE)
@@ -397,8 +411,30 @@
             pieces.append(lax.dynamic_index_in_dim(everything[:, slot], origin, 0, keepdims=False))
         return jnp.concatenate(pieces, axis=0)
 
+    own_rows = lax.dynamic_index_in_dim(
+        lower.reshape(first, side, TILE, first, side, TILE), row_index, 1, keepdims=False
+    )
+    own_corner = lax.dynamic_index_in_dim(own_rows, col_index, 3, keepdims=False)
+    own_below = lax.dynamic_index_in_dim(
+        row_factor.reshape(rest_rows, TILE, first, side, TILE), col_index, 3, keepdims=False
+    )
+    top = jnp.concatenate(
+        [own_corner, jnp.zeros((first, TILE, rest_cols, TILE), jnp.float32)], axis=2
+    )
+    bottom = jnp.concatenate(
+        [own_below, rest.reshape(rest_rows, TILE, rest_cols, TILE)], axis=2
+    )
+    factored = jnp.concatenate([top, bottom], axis=0).reshape(front.shape)
+    parent_local = parent[:, 0, 0, :, :, 0, :].reshape(-1, col_slots * TILE)
+    grouped, factored, parent_local = lax.optimization_barrier(
+        (by_groups(summed), factored, parent_local)
+    )
+
     even = jnp.all(sorted_shift == slots // share)
-    rotated = lax.cond(even, by_groups, by_gather, summed)
+    rotated = lax.cond(
+        even, lambda grouped, value: grouped, lambda grouped, value: by_gather(value),
+        grouped, summed,
+    )
 
     position = rank.reshape(-1, 2)
     across = place(
@@ -407,7 +443,6 @@
         jnp.arange(half, dtype=jnp.int32),
     )
     other = lax.ppermute(across, "leaf", swap)
-    parent_local = parent[:, 0, 0, :, :, 0, :].reshape(-1, col_slots * TILE)
     new_parent = add_rows(
         parent_local,
         rotated,
@@ -416,20 +451,6 @@
         leaf_index.astype(jnp.int32)[None],
     ).reshape(parent.shape)
 
-    own_rows = lax.dynamic_index_in_dim(
-        lower.reshape(first, side, TILE, first, side, TILE), row_index, 1, keepdims=False
-    )
-    own_corner = lax.dynamic_index_in_dim(own_rows, col_index, 3, keepdims=False)
-    own_below = lax.dynamic_index_in_dim(
-        row_factor.reshape(rest_rows, TILE, first, side, TILE), col_index, 3, keepdims=False
-    )
-    top = jnp.concatenate(
-        [own_corner, jnp.zeros((first, TILE, rest_cols, TILE), jnp.float32)], axis=2
-    )
-    bottom = jnp.concatenate(
-        [own_below, rest.reshape(rest_rows, TILE, rest_cols, TILE)], axis=2
-    )
-    factored = jnp.concatenate([top, bottom], axis=0).reshape(front.shape)
     return (factored, new_parent)
 
 

time: 722 us -> 697 us (0.965); the launches traced: 715 us -> 698 us
  local copies, waits for them, and re-layouts: 194 us -> 150 us
  waiting for transfers between devices: 271 us -> 281 us
    all_gather x1, waiting for transfers between devices: 37.9 us -> 147 us  [per_device_square(): leading = lax.all_gather(x[:first, :, :first, :], ('row', 'col'))]
    ppermute x3, waiting for transfers between devices: 179 us -> 120 us  [by_groups(): pieces.append(lax.ppermute(piece, 'row', perm))]
    all_gather x2 -> x1, waiting for transfers between devices: 52.5 us -> 0.01 us  [per_device_square(): panel_rows = lax.all_gather(panel_rows, 'col', axis=1, tiled=True)]
    all_gather x2 -> x0, local copies, waits for them, and re-layouts: 20.4 us -> none  [the longest x1 10.9 us: per_device_square(): panel_rows = lax.all_gather(x[first:, :, :first, :], 'col')]
    reshape x2 -> x0, local copies, waits for them, and re-layouts: 19.7 us -> none  [the longest x1 9.88 us: per_device_square(): panel_rows.transpose(1, 2, 3, 0, 4).reshape(rest_rows * TILE, NPIV)]
    reshape x1, local copies, waits for them, and re-layouts: 22.5 us -> 6.9 us  [per_device_square(): leading = leading.reshape(side, side, first, TILE, first, TILE)]
    pallas_call x1, Pallas kernels: 111 us -> 125 us  [factor_leading(): pl.pallas_call(factor_kernel, out_shape=(shape, shape), in_specs=[pl.Bloc...]
    concatenate x1 -> x0, other arithmetic: 11.9 us -> none  [per_device_square(): factored = jnp.concatenate([top, bottom], axis=0).reshape(front.shape)]
  transfers between devices with their start and end apart: 8 -> 10, of which waited for: 6 -> 5; matrix products, arithmetic and copies ran while one was open for 21% -> 19% of each run, Pallas kernels for 16% -> 18%
where the time goes in v2:
time: 697 us; the launch traced here: 698 us
  waiting for transfers between devices  281 us (40%)
  local copies, waits for them, and re-layouts  150 us (22%)
  Pallas kernels  140 us (20%)
  matrix products  68.8 us (10%)
  other arithmetic  30.7 us (4%)
  between operations  15.2 us (2%)
  starting transfers between devices  11.5 us (2%)
    all_gather x1, waiting for transfers between devices, per_device_square(): leading = lax.all_gather(x[:first, :, :first, :], ('row', 'col'))  147 us
    pallas_call x1, Pallas kernels, factor_leading(): pl.pallas_call(factor_kernel, out_shape=(shape, shape), in_specs=[pl.Bloc...  125 us
    ppermute x3, waiting for transfers between devices, by_groups(): pieces.append(lax.ppermute(piece, 'row', perm))  120 us
    unnamed x33, local copies, waits for them, and re-layouts  55.4 us
    dot_general x1, matrix products, per_device_square(): lax.dot_general(row_factor, col_factor, (((1,), (0,)), ((), ())), precisi...  34.6 us
    slice x2, local copies, waits for them, and re-layouts, per_device_square(): rest = x[first:, :, first:, :].reshape(rest_rows * TILE, rest_cols * TILE)  30.8 us
    dot_general x1, matrix products, per_device_square(): lax.dot_general(panel_rows, jnp.concatenate(by_col, axis=1), (((1,), (1,)...  17.5 us
    dot_general x1, matrix products, per_device_square(): lax.dot_general(jnp.concatenate(by_row, axis=1), panel_cols, (((1,), (0,)...  16.7 us
  transfers between devices with their start and end apart: 10, of which 5 were waited for; matrix products, arithmetic and copies ran while one was open for 19% of the time, Pallas kernels for 18%

profile of v2, /device:TPU:11, one launch (start us, length us, event | category | flops | bytes accessed | tf_op | source)
XLA Modules:
  0.0 697.8 jit_solution(615481160713705947)
XLA Ops:
  7.2 10.9 %copy.50 = f32[1,16,1,128,16,1,128]{6,3,4,1,5,2,0:T(8,128)S(1)} copy(f32[1,16,1,128,16,1,128]{6,5,4,3,2,1,0:T(1,128)} %param.6) | data formatting | bytes 33554432 | tf_op args[0]
  18.1 6.2 copy-done.5
  24.3 0.7 slice.177
  25.1 1.7 slice.178
  26.8 1.4 copy.32
  28.2 1.4 copy.54
  29.7 2.9 slice.179
  32.6 3.3 copy.33
  36.0 1.4 copy.53
  37.3 1.3 collective-permute-start.2
  38.6 1.0 collective-permute-start.1
  39.6 1.7 collective-permute-start
  41.3 11.5 %slice.176 = f32[14,128,14,128]{3,1,2,0:T(8,128)} slice(f32[16,128,16,128]{3,1,2,0:T(8,128)} %bitcast.108), slice={[2:16], [0:128], [2:16], [0:128]} | slice | bytes 25690112 | tf_op jit(solution)/shard_map/slice | solution.py:363
  53.0 0.2 dynamic-slice_reduce_fusion
  53.2 0.1 select_reduce_fusion.1
  53.4 19.3 %copy.30 = f32[14,128,14,128]{3,2,1,0:T(8,128)} copy(f32[14,128,14,128]{3,1,2,0:T(8,128)} %slice.176) | data formatting | bytes 25690112 | tf_op jit(solution)/shard_map/slice | solution.py:363
  72.7 0.2 convert_reduce_fusion
  72.9 0.1 select_reduce_fusion
  73.0 147.1 %all-gather.10.cloned.1.call-done = f32[32,128,2,128]{3,1,2,0:T(8,128)} async-done(((f32[2,128,2,128]{3,1,2,0:T(8,128)}), f32[32,128,2,128]{3,1,2,0:T(8,128)}) %all-gather.10.cloned.1.call-update) | async-done | bytes 4194320 | tf_op jit(solution)/shard_map/all_gather | solution.py:332
  220.1 6.9 copy.52
  227.0 5.5 reshape.97.a_ref
  232.5 125.2 %factor_leading.1 = (f32[1024,1024]{1,0:T(8,128)}, f32[1024,1024]{1,0:T(8,128)}) custom-call(f32[1024,1024]{1,0:T(8,128)} %reshape.97.a_ref), custom_call_target="tpu_custom_call" | custom-call | flops 4294967296 | bytes 12582912 | tf_op jit(solution)/shard_map/factor_leading/pallas_call | solution.py:244
  357.7 1.5 dynamic-slice_dynamic-update-slice_fusion.7
  359.2 1.4 dynamic-slice_dynamic-update-slice_fusion.6
  360.6 0.1 dynamic-slice_dynamic-update-slice_fusion.5
  360.8 0.2 dynamic-slice_dynamic-update-slice_fusion.4
  361.0 0.1 dynamic-slice_dynamic-update-slice_fusion.3
  361.1 0.2 dynamic-slice_dynamic-update-slice_fusion.2
  361.3 0.2 dynamic-slice_dynamic-update-slice_fusion.1
  361.5 0.1 dynamic-slice_dynamic-update-slice_fusion
  361.7 1.9 copy-done.8
  363.6 16.7 %fusion.1 = f32[1024,1792]{1,0:T(8,128)} fusion(f32[1024,1024]{1,0:T(8,128)S(1)} %get-tuple-element.79, f32[256,1792]{0,1:T(8,128)S(1)} %collective-permute-done.2, f32[256,1792]{0,1:T(8,128)} %collective-permute-done.1, f32[256,1792]{0,1:T(8,128)} %collective-permute-done, f32[256,1792]{0,1:T(8,128)} %bitcast.101), kind=kOutput, calls=%fused_computation.23 | convolution fusion | flops 11279794176 | bytes 18874368 | tf_op jit(solution)/shard_map/dot_general | solution.py:359
  380.3 17.5 %fusion.22 = f32[1024,1792]{1,0:T(8,128)} fusion(f32[1024,1024]{1,0:T(8,128)} %copy-done.8, f32[1792,1024]{1,0:T(8,128)} %all-gather.8.cloned.1.call-done), kind=kOutput, calls=%fused_computation.94 | convolution fusion | flops 11274289152 | bytes 18874368 | tf_op jit(solution)/shard_map/dot_general | solution.py:355
  397.8 34.6 %bitcast_subtract_fusion.source_ref = f32[1792,1792]{1,0:T(8,128)} fusion(f32[224,8,14,128]{3,2,1,0:T(8,128)} %bitcast.112, f32[1024,1792]{1,0:T(8,128)} %fusion.22, f32[1024,1792]{1,0:T(8,128)} %fusion.1), kind=kOutput, calls=%fused_computation.20 | convolution fusion | flops 19733217280 | bytes 40370176 | tf_op jit(solution)/shard_map/dot_general | solution.py:364
  432.4 4.6 copy-done.2
  437.1 2.0 place.4
  439.1 0.5 collective-permute-start.3
  439.5 2.0 place.3
  441.5 3.4 copy-done.4
  444.9 7.5 %collective-permute-done.3 = f32[2048,1024]{1,0:T(8,128)} collective-permute-done((f32[2048,1024]{1,0:T(8,128)S(1)}, f32[2048,1024]{1,0:T(8,128)}, u32[]{:S(2)}, u32[]{:S(2)}) %collective-permute-start.3) | collective-permute-done | bytes 8388640 | tf_op jit(solution)/shard_map/ppermute | solution.py:392
  452.4 12.0 %add.292 = f32[2048,1024]{1,0:T(8,128)} add(f32[2048,1024]{1,0:T(8,128)} %copy-done.4, f32[2048,1024]{1,0:T(8,128)} %collective-permute-done.3) | non-fusion elementwise | flops 2097152 | bytes 25165824 | tf_op jit(solution)/shard_map/add | solution.py:394
  464.4 7.5 %fusion.21 = (f32[512,1024]{1,0:T(8,128)}, f32[512,1024]{1,0:T(8,128)}, f32[512,1024]{1,0:T(8,128)}, f32[512,1024]{1,0:T(8,128)}) fusion(f32[2048,1024]{1,0:T(8,128)} %add.292), kind=kLoop, calls=%fused_computation.93 | loop fusion | bytes 16777216 | tf_op jit(solution)/shard_map/slice | solution.py:399
  471.9 0.9 collective-permute-start.6
  472.8 4.5 collective-permute-start.5
  477.4 0.2 collective-permute-start.4
  477.7 10.7 %copy.51 = f32[128,8,16,128]{3,1,2,0:T(8,128)} copy(f32[128,8,16,128]{3,2,1,0:T(8,128)} %bitcast.113) | data formatting | bytes 16777216
  488.4 0.6 compare_reduce_fusion
  489.6 0.2 fusion.14
  489.9 5.6 reshape.100
  495.5 1.5 constant_dynamic-slice_fusion.3
  497.0 15.0 %reshape.102 = f32[14,128,14,128]{3,2,1,0:T(8,128)} reshape(f32[1792,1792]{1,0:T(8,128)} %bitcast_subtract_fusion.source_ref) | data formatting | bytes 25690112 | tf_op jit(solution)/shard_map/reshape | solution.py:425
  512.0 9.2 %reshape.110 = f32[14,128,2,4,128]{1,0,4,3,2:T(8,128)} reshape(f32[1792,1024]{0,1:T(8,128)} %bitcast.118) | data formatting | bytes 14680064 | tf_op jit(solution)/shard_map/reshape | solution.py:419
  521.2 1.7 constant_dynamic-slice_fusion.2
  523.0 2.3 copy.38
  525.3 11.9 %fusion = f32[1,16,1,128,16,1,128]{6,4,3,1,5,2,0:T(8,128)} fusion(f32[2,128,2,128]{3,2,1,0:T(2,128)S(1)} %bitcast.121, f32[14,128,14,128]{3,2,1,0:T(8,128)} %reshape.102, f32[14,128,2,128]{3,2,1,0:T(2,128)} %bitcast.119), kind=kLoop, calls=%fused_computation.17 | loop fusion | flops 16777216 | bytes 31719424 | tf_op jit(solution)/shard_map/reshape | solution.py:427
  537.2 115.4 %collective-permute-done.5 = f32[512,1024]{1,0:T(8,128)} collective-permute-done((f32[512,1024]{1,0:T(8,128)}, f32[512,1024]{1,0:T(8,128)}, u32[]{:S(2)}, u32[]{:S(2)}) %collective-permute-start.5) | collective-permute-done | bytes 2097184 | tf_op jit(solution)/shard_map/ppermute | solution.py:403
  652.6 4.4 collective-permute-done.4
  657.0 5.8 pad_maximum_fusion
  662.8 5.4 place.5
  668.2 1.3 collective-permute-start.7
  669.5 6.8 collective-permute-done.7.other_ref
  676.3 3.4 copy-done.3
  679.7 5.7 add_rows.1
  685.4 5.4 copy.43
  (34 shorter events, 0.5 us)
Async XLA Ops:
  7.2 45.7 %copy-start = (s32[2,56]{1,0:T(2,128)S(1)}, s32[2,56]{1,0:T(2,128)}, u32[]{:S(2)}) copy-start(s32[2,56]{1,0:T(2,128)} %param.8) | copy-start | bytes 1348
  7.2 213.0 %all-gather.10.cloned.1.call-start = ((), (), s32[]{:S(2)}) async-start(), calls=%async_computation.2 | async-start | bytes 4456448 | tf_op jit(solution)/shard_map/all_gather | solution.py:332
  18.1 6.2 copy-start.5
  25.0 355.3 %all-gather.8.cloned.1.call-start = ((), (), s32[]{:S(2)}) async-start(), calls=%async_computation.1 | async-start | bytes 9175040 | tf_op jit(solution)/shard_map/all_gather | solution.py:336
  37.3 326.3 %collective-permute-start.2 = (f32[256,1792]{0,1:T(8,128)}, f32[256,1792]{0,1:T(8,128)S(1)}, u32[]{:S(2)}, u32[]{:S(2)}) collective-permute-start(f32[256,1792]{0,1:T(8,128)} %bitcast.101), channel_id=1, source_target_pairs={{0,4},{4,8},{8,12},{12,0},{1,5},{5,9},{9,13},{13,1},{2,6},{6,10},{... | collective-permute-start | bytes 5505032 | tf_op jit(solution)/shard_map/ppermute | solution.py:341
  38.6 325.0 %collective-permute-start.1 = (f32[256,1792]{0,1:T(8,128)}, f32[256,1792]{0,1:T(8,128)}, u32[]{:S(2)}, u32[]{:S(2)}) collective-permute-start(f32[256,1792]{0,1:T(8,128)} %bitcast.101), channel_id=1, source_target_pairs={{0,8},{4,12},{8,0},{12,4},{1,9},{5,13},{9,1},{13,5},{2,10},{6,14},... | collective-permute-start | bytes 5505032 | tf_op jit(solution)/shard_map/ppermute | solution.py:341
  39.6 324.0 %collective-permute-start = (f32[256,1792]{0,1:T(8,128)}, f32[256,1792]{0,1:T(8,128)}, u32[]{:S(2)}, u32[]{:S(2)}) collective-permute-start(f32[256,1792]{0,1:T(8,128)} %bitcast.101), channel_id=1, source_target_pairs={{0,12},{4,0},{8,4},{12,8},{1,13},{5,1},{9,5},{13,9},{2,14},{6,2},{... | collective-permute-start | bytes 5505032 | tf_op jit(solution)/shard_map/ppermute | solution.py:341
  53.4 19.3 %copy-start.9 = (s32[16]{0:T(128)S(1)}, s32[16]{0:T(128)}, u32[]{:S(2)}) copy-start(s32[16]{0:T(128)} %param.9) | copy-start | bytes 196
  357.7 2.9 copy-start.6
  361.7 1.9 copy-start.8
  432.4 4.7 copy-start.2
  439.1 13.4 %collective-permute-start.3 = (f32[2048,1024]{1,0:T(8,128)S(1)}, f32[2048,1024]{1,0:T(8,128)}, u32[]{:S(2)}, u32[]{:S(2)}) collective-permute-start(f32[2048,1024]{1,0:T(8,128)S(1)} %place.4), channel_id=1, source_target_pairs={{0,16},{16,0},{1,17},{17,1},{2,18},{18,2},{3,19},{19,3},{4,20},{20... | collective-permute-start | bytes 25165832 | tf_op jit(solution)/shard_map/ppermute | solution.py:392
  441.5 3.4 copy-start.4
  471.9 65.3 %collective-permute-start.6 = (f32[512,1024]{1,0:T(8,128)}, f32[512,1024]{1,0:T(8,128)}, u32[]{:S(2)}, u32[]{:S(2)}) collective-permute-start(f32[512,1024]{1,0:T(8,128)} %get-tuple-element.76), channel_id=1, source_target_pairs={{0,4},{4,8},{8,12},{12,0},{1,5},{5,9},{9,13},{13,1},{2,6},{6,10},{... | collective-permute-start | bytes 6291464 | tf_op jit(solution)/shard_map/ppermute | solution.py:403
  472.8 179.8 %collective-permute-start.5 = (f32[512,1024]{1,0:T(8,128)}, f32[512,1024]{1,0:T(8,128)}, u32[]{:S(2)}, u32[]{:S(2)}) collective-permute-start(f32[512,1024]{1,0:T(8,128)} %get-tuple-element.77), channel_id=1, source_target_pairs={{0,8},{4,12},{8,0},{12,4},{1,9},{5,13},{9,1},{13,5},{2,10},{6,14},... | collective-permute-start | bytes 6291464 | tf_op jit(solution)/shard_map/ppermute | solution.py:403
  477.4 179.7 %collective-permute-start.4 = (f32[512,1024]{1,0:T(8,128)}, f32[512,1024]{1,0:T(8,128)}, u32[]{:S(2)}, u32[]{:S(2)}) collective-permute-start(f32[512,1024]{1,0:T(8,128)} %get-tuple-element.78), channel_id=1, source_target_pairs={{0,12},{4,0},{8,4},{12,8},{1,13},{5,1},{9,5},{13,9},{2,14},{6,2},{... | collective-permute-start | bytes 6291464 | tf_op jit(solution)/shard_map/ppermute | solution.py:403
  525.3 131.8 %copy-start.7 = (f32[512,1024]{1,0:T(8,128)S(1)}, f32[512,1024]{1,0:T(8,128)}, u32[]{:S(2)}) copy-start(f32[512,1024]{1,0:T(8,128)} %get-tuple-element.75) | copy-start | bytes 6291460
  668.2 8.1 %collective-permute-start.7 = (f32[1024,1024]{1,0:T(8,128)S(1)}, f32[1024,1024]{1,0:T(8,128)S(1)}, u32[]{:S(2)}, u32[]{:S(2)}) collective-permute-start(f32[1024,1024]{1,0:T(8,128)S(1)} %place.5), channel_id=1, source_target_pairs={{0,16},{16,0},{1,17},{17,1},{2,18},{18,2},{3,19},{19,3},{4,20},{20... | collective-permute-start | bytes 12582920 | tf_op jit(solution)/shard_map/ppermute | solution.py:445
  676.3 3.4 copy-start.3
  685.4 5.4 copy-start.1
Sparse Core Ops, SparseCore 0:
  25.2 194.9 all-gather.9
  222.0 81.1 all-gather.7
